TPU v7x, 32 devices: a whole 2x2x4 slice. The times are simulated.
32 devices in a mesh: ctx: 8 (over z, y), head: 4 (over x, core).
Axes of the slice: x: 2, y: 2, z: 4, core: 2. Of those that a mesh axis runs over, the one named last changes fastest.
Arguments:
- queries: bfloat16 [2048, 2048], P('ctx', 'head'), may hold values from -34 to 34
- keys: bfloat16 [2048, 2048], P('ctx', 'head'), may hold values from -34 to 34
- values: bfloat16 [2048, 2048], P('ctx', 'head'), may hold values from -6 to 6
- output_grad: bfloat16 [2048, 4096], P('ctx', 'head'), may hold values from -6 to 6
- out_weight: bfloat16 [2048, 4096], P('head'), may hold values from -0.125 to 0.125
- random_blocks: int32 [16, 32, 3], replicated, may hold values from 0 to 31, as said below
- global_blocks: int32 [2], replicated, may hold values from 0 to 31, as said below
Outputs:
- output: bfloat16 [2048, 4096], P('ctx', 'head')
- query_grad: bfloat16 [2048, 2048], P('ctx', 'head')
- key_grad: bfloat16 [2048, 2048], P('ctx', 'head')
- value_grad: bfloat16 [2048, 2048], P('ctx', 'head')
Inputs may be any that keep to these rules, and one draw needn't show every extreme that they name: Every entry random_blocks[h, i, r] names a block j with j // 4 != i // 4. For each group of 4 heads (heads g * 4 to (g + 1) * 4 - 1) and each aligned run of 4 query blocks, the 48 entries name blocks of any one other run at most 7 times, and of some run exactly 7 times. `global_blocks`: the 2 entries are distinct, and one of them is the last block.
All inputs are finite; a program needn't handle non-finite values.
Results may differ from a plain program's by a relative error of at most 0.027.
Values may be sent and summed in bfloat16 or wider, within the bound.
A program may use at most 128 MiB of HBM per device.

v0:
```python
import jax
import jax.numpy as jnp
from jax import lax
from jax.sharding import PartitionSpec as P

HD = 128
BLK = 64
R = 3
G = 2


def with_halo(cells, sides, width):
    for axis, dim in sides:
        count = lax.axis_size(axis)
        ends = count - 1
        head = lax.slice_in_dim(cells, 0, width, axis=dim)
        tail = lax.slice_in_dim(cells, cells.shape[dim] - width, cells.shape[dim], axis=dim)
        cells = jnp.concatenate(
            [
                lax.ppermute(tail, axis, [(i, (i + 1) % count) for i in range(ends)]),
                cells,
                lax.ppermute(head, axis, [((i + 1) % count, i) for i in range(ends)]),
            ],
            axis=dim,
        )
    return cells


def send_plan(request_table, shards, blocks, my_shard):
    requests = request_table.shape[1]
    owners = request_table // blocks
    within = request_table % blocks
    request_ids = jnp.arange(requests, dtype=jnp.int32)
    earlier = (owners[:, :, None] == owners[:, None, :]) & (
        request_ids[None, None, :] < request_ids[None, :, None]
    )
    ranking = jnp.sum(earlier.astype(jnp.int32), axis=2)
    capacity = (requests + shards - 2) // (shards - 1)
    slot_ids = jnp.arange(capacity, dtype=jnp.int32)
    owned = (owners == my_shard)[:, None, :] & (ranking[:, None, :] == slot_ids[None, :, None])
    tile_ids = (request_ids // (blocks * R))[None, :] * blocks + within
    send_tiles = jnp.sum(jnp.where(owned, tile_ids[:, None, :], 0), axis=2).reshape(-1)
    send_alive = jnp.any(owned, axis=2).reshape(-1)
    my_owners = lax.dynamic_index_in_dim(owners, my_shard, 0, keepdims=False)
    my_ranks = lax.dynamic_index_in_dim(ranking, my_shard, 0, keepdims=False)
    return (send_tiles, send_alive, my_owners * capacity + my_ranks)


def pick_tiles(pair_tiles, send_tiles, blocks):
    return pair_tiles[send_tiles % blocks, :, send_tiles // blocks, :]


def pair_products(row_tiles, window, global_pairs, fetched, low_edge, high_edge):
    nearby = jnp.einsum(
        "nqhd,nwbhd->nhqwb",
        row_tiles,
        window[..., low_edge:high_edge],
        preferred_element_type=jnp.float32,
    )
    distant = jnp.einsum(
        "nqhd,gbhd->nhqgb",
        row_tiles,
        global_pairs[..., low_edge:high_edge],
        preferred_element_type=jnp.float32,
    )
    chance = jnp.einsum(
        "nqhd,hnrbd->nhqrb",
        row_tiles,
        fetched[..., low_edge:high_edge],
        preferred_element_type=jnp.float32,
    )
    return jnp.concatenate([nearby, distant, chance], axis=3)


def collect_rows(mixing, window, global_pairs, fetched, low_edge, high_edge):
    nearby = jnp.einsum(
        "nhqwb,nwbhd->nqhd",
        mixing[:, :, :, :3],
        window[..., low_edge:high_edge],
        preferred_element_type=jnp.float32,
    )
    distant = jnp.einsum(
        "nhqgb,gbhd->nqhd",
        mixing[:, :, :, 3 : 3 + G],
        global_pairs[..., low_edge:high_edge],
        preferred_element_type=jnp.float32,
    )
    chance = jnp.einsum(
        "nhqrb,hnrbd->nqhd",
        mixing[:, :, :, 3 + G :],
        fetched[..., low_edge:high_edge],
        preferred_element_type=jnp.float32,
    )
    return nearby + distant + chance


def tile_terms(mixing, row_tiles):
    nearby = jnp.einsum(
        "nhqwb,nqhd->nwbhd", mixing[:, :, :, :3], row_tiles, preferred_element_type=jnp.float32
    )
    distant = jnp.einsum(
        "nhqgb,nqhd->gbhd",
        mixing[:, :, :, 3 : 3 + G],
        row_tiles,
        preferred_element_type=jnp.float32,
    )
    chance = jnp.einsum(
        "nhqrb,nqhd->hnrbd", mixing[:, :, :, 3 + G :], row_tiles, preferred_element_type=jnp.float32
    )
    return (nearby, distant, chance)


def body(queries, keys, values, output_grad, out_weight, random_blocks, global_blocks):
    shards = lax.axis_size("ctx")
    my_shard = lax.axis_index("ctx")
    head_group = lax.axis_index("head")
    tok_local, width_local = queries.shape
    head_dim = HD
    heads_local = width_local // head_dim
    blocks = tok_local // BLK
    scaling = head_dim ** (-0.5)
    query_tiles = queries.reshape(blocks, BLK, heads_local, head_dim)
    pair_tiles = jnp.concatenate(
        [
            keys.reshape(blocks, BLK, heads_local, head_dim),
            values.reshape(blocks, BLK, heads_local, head_dim),
        ],
        axis=3,
    )
    head_table = lax.dynamic_slice_in_dim(random_blocks, head_group * heads_local, heads_local, 0)
    request_table = (
        head_table.reshape(heads_local, shards, blocks, R)
        .transpose(1, 0, 2, 3)
        .reshape(shards, heads_local * blocks * R)
    )
    send_tiles, send_alive, receive_rows = send_plan(request_table, shards, blocks, my_shard)
    received = lax.all_to_all(
        pick_tiles(pair_tiles, send_tiles, blocks), "ctx", split_axis=0, concat_axis=0, tiled=True
    )
    fetched = received[receive_rows].reshape(heads_local, blocks, R, BLK, 2 * head_dim)
    padded = with_halo(pair_tiles.reshape(tok_local, 2 * width_local), (("ctx", 0),), BLK)
    padded = padded.reshape(blocks + 2, BLK, heads_local, 2 * head_dim)
    window = jnp.stack([padded[offset : offset + blocks] for offset in range(3)], axis=1)
    global_owner = global_blocks // blocks
    global_local = global_blocks % blocks
    picked = pair_tiles[global_local]
    holding = jnp.where(
        (global_owner == my_shard)[:, None, None, None], picked.astype(jnp.float32), 0.0
    )
    global_pairs = lax.psum(holding, "ctx").astype(jnp.bfloat16)
    first_block = my_shard * blocks
    window_ids = first_block + jnp.arange(blocks)[:, None] + jnp.arange(3)[None, :] - 1
    inside = (window_ids >= 0) & (window_ids < blocks * shards)
    alive_mask = jnp.concatenate([inside, jnp.ones((blocks, G + R), dtype=bool)], axis=1)[
        :, None, None, :, None
    ]
    logits = jnp.where(
        alive_mask,
        pair_products(query_tiles, window, global_pairs, fetched, 0, head_dim) * scaling,
        -jnp.inf,
    )
    row_max = jnp.max(logits, axis=(3, 4))
    log_total = row_max + jnp.log(jnp.sum(jnp.exp(logits - row_max[..., None, None]), axis=(3, 4)))
    weights_full = jnp.exp(logits - log_total[..., None, None])
    weights_low = weights_full.astype(jnp.bfloat16)
    attended = collect_rows(
        weights_low, window, global_pairs, fetched, head_dim, 2 * head_dim
    ).astype(jnp.bfloat16)
    attended_flat = attended.reshape(tok_local, width_local)
    partial_value = jnp.dot(attended_flat, out_weight, preferred_element_type=jnp.float32)
    output = lax.psum_scatter(partial_value, "head", scatter_dimension=1, tiled=True).astype(
        jnp.bfloat16
    )
    grad_sum = lax.dot_general(
        lax.all_gather(output_grad, "head", axis=1, tiled=True),
        out_weight,
        (((1,), (1,)), ((), ())),
        preferred_element_type=jnp.float32,
    )
    grad_tiles = grad_sum.astype(jnp.bfloat16).reshape(blocks, BLK, heads_local, head_dim)
    delta_rows = jnp.sum(
        grad_tiles.astype(jnp.float32) * attended.astype(jnp.float32), axis=3
    ).transpose(0, 2, 1)
    products = pair_products(grad_tiles, window, global_pairs, fetched, head_dim, 2 * head_dim)
    logit_grad = (weights_full * (products - delta_rows[..., None, None])).astype(jnp.bfloat16)
    query_grad = (
        (collect_rows(logit_grad, window, global_pairs, fetched, 0, head_dim) * scaling)
        .astype(jnp.bfloat16)
        .reshape(tok_local, width_local)
    )
    key_nearby, key_distant, key_chance = tile_terms(logit_grad, query_tiles)
    value_nearby, value_distant, value_chance = tile_terms(weights_low, grad_tiles)
    nearby_terms = jnp.concatenate([key_nearby * scaling, value_nearby], axis=4)
    framed = sum(
        (
            jnp.pad(nearby_terms[:, offset], ((offset, 2 - offset), (0, 0), (0, 0), (0, 0)))
            for offset in range(3)
        )
    )
    edge_rows = jnp.concatenate([framed[0], framed[blocks + 1]], axis=0).reshape(
        2 * BLK, 2 * width_local
    )
    arrived = with_halo(edge_rows.astype(jnp.bfloat16), (("ctx", 0),), BLK).astype(edge_rows.dtype)
    local_grad = framed[1 : blocks + 1]
    local_grad = local_grad.at[0].add(arrived[:BLK].reshape(BLK, heads_local, 2 * head_dim))
    local_grad = local_grad.at[blocks - 1].add(
        arrived[3 * BLK :].reshape(BLK, heads_local, 2 * head_dim)
    )
    distant_terms = jnp.concatenate([key_distant * scaling, value_distant], axis=3)
    summed = lax.psum(distant_terms, "ctx")
    selector = (
        (global_owner == my_shard)[:, None] & (global_local[:, None] == jnp.arange(blocks)[None, :])
    ).astype(jnp.float32)
    local_grad = local_grad + jnp.einsum(
        "gn,gbhd->nbhd", selector, summed, precision=lax.Precision.HIGHEST
    )
    chance_terms = (
        jnp.concatenate([key_chance * scaling, value_chance], axis=4)
        .astype(jnp.bfloat16)
        .reshape(-1, BLK, 2 * head_dim)
    )
    outgoing_grads = (
        jnp.zeros((send_tiles.shape[0], BLK, 2 * head_dim), jnp.bfloat16)
        .at[receive_rows]
        .set(chance_terms)
    )
    returned = lax.all_to_all(outgoing_grads, "ctx", split_axis=0, concat_axis=0, tiled=True)
    segment_ids = jnp.where(send_alive, send_tiles, heads_local * blocks)
    gathered = jax.ops.segment_sum(
        returned.astype(jnp.float32), segment_ids, num_segments=heads_local * blocks + 1
    )[: heads_local * blocks]
    local_grad = local_grad + gathered.reshape(heads_local, blocks, BLK, 2 * head_dim).transpose(
        1, 2, 0, 3
    )
    key_grad = local_grad[..., :head_dim].astype(jnp.bfloat16).reshape(tok_local, width_local)
    value_grad = local_grad[..., head_dim:].astype(jnp.bfloat16).reshape(tok_local, width_local)
    return (output, query_grad, key_grad, value_grad)


def solution(mesh):
    placed = (
        P("ctx", "head"),
        P("ctx", "head"),
        P("ctx", "head"),
        P("ctx", "head"),
        P("head", None),
        P(),
        P(),
    )
    return jax.shard_map(
        body,
        mesh=mesh,
        in_specs=placed,
        out_specs=(P("ctx", "head"), P("ctx", "head"), P("ctx", "head"), P("ctx", "head")),
        check_vma=False,
    )
```

profile of v0, /device:TPU:0, one launch (start us, length us, event | category | flops | bytes accessed | tf_op | source)
XLA Modules:
  0.0 266.9 jit_solution(3460373470147299995)
XLA Ops:
  7.2 0.7 all-gather.2.cloned.1.call-update
  9.5 1.0 reshape.465
  10.6 1.0 reshape.466
  11.7 2.1 gather_fusion.1
  13.8 7.4 %all-to-all-start = ((bf16[56,64,256]{2,1,0:T(8,128)(2,1)}), bf16[56,64,256]{2,1,0:T(8,128)(2,1)}, u32[]{:S(2)}, u32[]{:S(2)}) async-start(bf16[56,64,256]{2,1,0:T(8,128)(2,1)} %gather_fusion.1), calls=%async_computation | async-start | bytes 3670016 | tf_op jit(solution)/shard_map/all_to_all | solution.py:137
  21.5 3.9 %collective-permute-start = (bf16[64,1024]{1,0:T(8,128)(2,1)S(1)}, bf16[64,1024]{1,0:T(8,128)(2,1)S(1)}, u32[]{:S(2)}, u32[]{:S(2)}) collective-permute-start(bf16[64,1024]{1,0:T(8,128)(2,1)S(1)} %bitcast.209), channel_id=1, source_target_pairs={{0,4},{4,8},{8,12},{12,16},{16,20},{20,24},{24,28},{1,5},{5,9},{9,... | collective-permute-start | bytes 393224 | tf_op jit(solution)/shard_map/ppermute | solution.py:20
  25.5 1.3 collective-permute-start.1
  26.9 0.6 gather_fusion
  27.7 69.8 %all-reduce.8 = bf16[2,64,4,256]{3,1,2,0:T(8,128)(2,1)S(1)} all-reduce(f32[2,64,4,256]{3,1,2,0:T(8,128)S(1)} %convert_select_fusion), channel_id=1, replica_groups=mesh['ctx'=8,'head'=4] {'ctx'}, use_global_device_ids=true, to_apply=%region_0.1 | all-reduce | flops 131072 | bytes 786432 | tf_op jit(solution)/shard_map/psum | solution.py:150
  97.5 0.7 fusion.100
  99.2 0.6 copy-done.22
  99.9 0.7 copy-done.23
  100.5 1.1 pad_maximum_fusion.4
  102.8 1.1 copy-done.6
  104.3 4.1 %convolution_convert_fusion.1 = bf16[256,512]{1,0:T(8,128)(2,1)S(1)} fusion(bf16[256,4096]{1,0:T(8,128)(2,1)} %all-gather.2.cloned.1.call-done, bf16[512,4096]{1,0:T(8,128)(2,1)} %param.15), kind=kOutput, calls=%fused_computation.40 | convolution fusion | flops 1073872896 | bytes 6553600 | tf_op jit(solution)/shard_map/dot_general | solution.py:174
  108.5 1.4 convolution_bitcast_fusion.2
  109.9 2.7 fusion.22
  112.5 3.4 %gather_fusion.2 = bf16[48,64,256]{2,1,0:T(8,128)(2,1)} fusion(bf16[56,64,256]{2,1,0:T(8,128)(2,1)} %all-to-all-done, s32[1024]{0:T(1024)S(1)} %pad_clamp_fusion), kind=kCustom, calls=%fused_computation.2 | custom fusion | bytes 3145920 | tf_op jit(solution)/shard_map/gather | solution.py:140
  115.9 1.6 fusion.96
  117.5 0.9 copy-done.12
  118.8 0.8 fusion.93
  119.6 1.3 exponential_reduce_fusion
  120.9 1.1 fusion.3
  123.9 1.1 multiply_reduce_fusion
  125.3 1.5 fusion.2
  126.9 1.4 copy-done.2
  128.6 0.8 pad_maximum_fusion.5
  129.9 5.4 %fusion.34 = f32[256,4096]{1,0:T(8,128)} fusion(bf16[512,4096]{1,0:T(8,128)(2,1)} %param.15, bf16[32,8,4,128]{3,2,1,0:T(4,128)(2,1)S(1)} %bitcast.194), kind=kOutput, calls=%fused_computation.76 | convolution fusion | flops 1073741824 | bytes 8650752 | tf_op jit(solution)/shard_map/dot_general | solution.py:170
  135.4 1.6 copy-done.3
  137.3 1.2 copy-done.5
  139.0 1.4 pad_maximum_fusion.1
  140.4 1.5 broadcast_in_dim.82
  141.8 7.7 %scatter_fusion = bf16[56,64,256]{2,1,0:T(8,128)(2,1)} fusion(bf16[56,64,256]{2,1,0:T(8,128)(2,1)} %broadcast_in_dim.82, s32[48]{0:T(128)S(1)} %fusion.85, bf16[48,64,256]{2,1,0:T(8,128)(2,1)} %pad_maximum_fusion.1), kind=kCustom, calls=%fused_computation.3 | custom fusion | bytes 4718784 | tf_op jit(solution)/shard_map/scatter | solution.py:225
  149.5 4.5 %all-to-all-start.1 = ((bf16[56,64,256]{2,1,0:T(8,128)(2,1)}), bf16[56,64,256]{2,1,0:T(8,128)(2,1)}, u32[]{:S(2)}, u32[]{:S(2)}) async-start(bf16[56,64,256]{2,1,0:T(8,128)(2,1)} %scatter_fusion), calls=%async_computation.2 | async-start | bytes 3670016 | tf_op jit(solution)/shard_map/all_to_all | solution.py:227
  155.5 4.1 %collective-permute-start.2 = (bf16[64,1024]{1,0:T(8,128)(2,1)S(1)}, bf16[64,1024]{1,0:T(8,128)(2,1)S(1)}, u32[]{:S(2)}, u32[]{:S(2)}) collective-permute-start(bf16[64,1024]{1,0:T(8,128)(2,1)S(1)} %bitcast.203), channel_id=1, source_target_pairs={{0,4},{4,8},{8,12},{12,16},{16,20},{20,24},{24,28},{1,5},{5,9},{9,... | collective-permute-start | bytes 393224 | tf_op jit(solution)/shard_map/ppermute | solution.py:20
  159.7 1.4 collective-permute-start.3
  162.7 0.7 copy.353
  163.5 6.2 %collective-permute-done.2 = bf16[64,1024]{1,0:T(8,128)(2,1)S(1)} collective-permute-done((bf16[64,1024]{1,0:T(8,128)(2,1)S(1)}, bf16[64,1024]{1,0:T(8,128)(2,1)S(1)}, u32[]{:S(2)}, u32[]{:S(2)}) %collective-permute-start.2) | collective-permute-done | bytes 131104 | tf_op jit(solution)/shard_map/ppermute | solution.py:20
  169.7 2.7 collective-permute-done.3
  172.7 1.0 fusion.38
  173.8 38.0 %all-reduce.7.cloned.1.call-done = f32[2,64,4,256]{3,1,2,0:T(8,128)} async-done(((f32[2,64,4,256]{3,1,2,0:T(8,128)}), f32[2,64,4,256]{3,1,2,0:T(8,128)}) %all-reduce.7.cloned.1.call-update) | async-done | bytes 524304 | tf_op jit(solution)/shard_map/psum | solution.py:210
  211.7 2.6 fusion.32
  214.3 3.8 %convert_element_type.63 = f32[56,64,256]{2,1,0:T(8,128)} convert(bf16[56,64,256]{2,1,0:T(8,128)(2,1)} %all-to-all-done.1) | non-fusion elementwise | flops 917504 | bytes 5505024 | tf_op jit(solution)/shard_map/convert_element_type | solution.py:230
  218.2 9.1 %scatter_fusion.1 = f32[17,64,256]{2,1,0:T(8,128)S(1)} fusion(f32[17,64,256]{2,1,0:T(8,128)S(1)} %broadcast_in_dim.80, s32[56]{0:T(128)S(1)} %get-tuple-element.53, f32[56,64,256]{2,1,0:T(8,128)} %convert_element_type.63), kind=kCustom, calls=%fused_computation.4 | custom fusion | flops 917504 | bytes 11010272 | tf_op jit(solution)/shard_map/scatter-add | solution.py:229
  227.4 0.8 fusion.16
  228.7 0.9 copy_bitcast_fusion
  229.6 28.7 %reduce-scatter.2.cloned.1.call-done = f32[256,1024]{1,0:T(8,128)} async-done(((f32[256,4096]{1,0:T(8,128)}), f32[256,1024]{1,0:T(8,128)}) %reduce-scatter.2.cloned.1.call-update) | async-done | bytes 1048592 | tf_op jit(solution)/shard_map/reduce_scatter | solution.py:171
  258.3 2.1 convert_element_type.56
  (132 shorter events, 13.1 us)
Async XLA Ops:
  7.2 0.8 copy-start
  7.2 97.1 %all-gather.2.cloned.1.call-start = ((), (), s32[]{:S(2)}) async-start(), calls=%async_computation.4 | async-start | bytes 2621440 | tf_op jit(solution)/shard_map/all_gather | solution.py:175
  13.8 13.0 %copy-start.24 = (s32[2]{0:T(128)S(1)}, s32[2]{0:T(128)}, u32[]{:S(2)}) copy-start(s32[2]{0:T(128)} %param.17) | copy-start | bytes 28
  13.8 13.0 %copy-start.21 = (bf16[256,512]{1,0:T(8,128)(2,1)S(1)}, bf16[256,512]{1,0:T(8,128)(2,1)}, u32[]{:S(2)}) copy-start(bf16[256,512]{1,0:T(8,128)(2,1)} %param.11) | copy-start | bytes 786436
  13.8 98.7 %all-to-all-start = ((bf16[56,64,256]{2,1,0:T(8,128)(2,1)}), bf16[56,64,256]{2,1,0:T(8,128)(2,1)}, u32[]{:S(2)}, u32[]{:S(2)}) async-start(bf16[56,64,256]{2,1,0:T(8,128)(2,1)} %gather_fusion.1), calls=%async_computation | async-start | bytes 3670016 | tf_op jit(solution)/shard_map/all_to_all | solution.py:137
  21.2 190.5 %all-reduce.7.cloned.1.call-start = ((), (), s32[]{:S(2)}) async-start(), calls=%async_computation.5 | async-start | bytes 1048576 | tf_op jit(solution)/shard_map/psum | solution.py:210
  21.5 77.7 %collective-permute-start = (bf16[64,1024]{1,0:T(8,128)(2,1)S(1)}, bf16[64,1024]{1,0:T(8,128)(2,1)S(1)}, u32[]{:S(2)}, u32[]{:S(2)}) collective-permute-start(bf16[64,1024]{1,0:T(8,128)(2,1)S(1)} %bitcast.209), channel_id=1, source_target_pairs={{0,4},{4,8},{8,12},{12,16},{16,20},{20,24},{24,28},{1,5},{5,9},{9,... | collective-permute-start | bytes 393224 | tf_op jit(solution)/shard_map/ppermute | solution.py:20
  25.5 73.7 %collective-permute-start.1 = (bf16[64,1024]{1,0:T(8,128)(2,1)S(1)}, bf16[64,1024]{1,0:T(8,128)(2,1)S(1)}, u32[]{:S(2)}, u32[]{:S(2)}) collective-permute-start(bf16[64,1024]{1,0:T(8,128)(2,1)S(1)} %bitcast.210), channel_id=1, source_target_pairs={{4,0},{8,4},{12,8},{16,12},{20,16},{24,20},{28,24},{5,1},{9,5},{13... | collective-permute-start | bytes 393224 | tf_op jit(solution)/shard_map/ppermute | solution.py:22
  26.9 75.8 %copy-start.9 = (bf16[4,64,4,128]{3,2,1,0:T(4,128)(2,1)}, bf16[4,64,4,128]{3,2,1,0:T(4,128)(2,1)S(1)}, u32[]{:S(2)}) copy-start(bf16[4,64,4,128]{3,2,1,0:T(4,128)(2,1)S(1)} %reshape.468) | copy-start | bytes 786436
  98.2 0.8 copy-start.18
  99.2 0.7 copy-start.22
  99.9 0.7 copy-start.23
  102.7 1.1 copy-start.6
  104.2 4.3 %copy-start.17 = (bf16[2,64,4,128]{3,1,2,0:T(8,128)(2,1)S(1)}, bf16[2,64,4,128]{3,1,2,0:T(8,128)(2,1)}, u32[]{:S(2)}) copy-start(bf16[2,64,4,128]{3,1,2,0:T(8,128)(2,1)} %get-tuple-element.51) | copy-start | bytes 393220
  115.9 2.5 copy-start.10
  117.5 0.9 copy-start.12
  120.9 1.4 copy-start.7
  122.3 1.5 copy-start.4
  123.5 1.4 copy-start.14
  123.5 1.8 copy-start.16
  126.9 1.4 copy-start.2
  128.3 1.4 copy-start.20
  129.4 128.8 %reduce-scatter.2.cloned.1.call-start = ((), (), s32[]{:S(2)}) async-start(), calls=%async_computation.3 | async-start | bytes 5242880 | tf_op jit(solution)/shard_map/reduce_scatter | solution.py:171
  135.3 1.6 copy-start.3
  135.3 1.6 copy-start.11
  136.9 1.6 copy-start.5
  149.5 64.8 %all-to-all-start.1 = ((bf16[56,64,256]{2,1,0:T(8,128)(2,1)}), bf16[56,64,256]{2,1,0:T(8,128)(2,1)}, u32[]{:S(2)}, u32[]{:S(2)}) async-start(bf16[56,64,256]{2,1,0:T(8,128)(2,1)} %scatter_fusion), calls=%async_computation.2 | async-start | bytes 3670016 | tf_op jit(solution)/shard_map/all_to_all | solution.py:227
  155.0 6.2 %copy-start.8 = (bf16[4,3,64,4,256]{4,2,1,3,0:T(8,128)(2,1)S(1)}, bf16[4,3,64,4,256]{4,2,1,3,0:T(8,128)(2,1)}, u32[]{:S(2)}) copy-start(bf16[4,3,64,4,256]{4,2,1,3,0:T(8,128)(2,1)} %copy-done.6) | copy-start | bytes 4718596
  155.3 7.1 %copy-start.15 = (f32[6,64,4,256]{3,1,2,0:T(8,128)}, f32[6,64,4,256]{3,1,2,0:T(8,128)S(1)}, u32[]{:S(2)}) copy-start(f32[6,64,4,256]{3,1,2,0:T(8,128)S(1)} %get-tuple-element.29) | copy-start | bytes 4718596
  155.3 6.3 %copy-start.13 = (bf16[4,4,3,64,128]{4,3,2,1,0:T(8,128)(2,1)S(1)}, bf16[4,4,3,64,128]{4,3,2,1,0:T(8,128)(2,1)}, u32[]{:S(2)}) copy-start(bf16[4,4,3,64,128]{4,3,2,1,0:T(8,128)(2,1)} %copy-done.12) | copy-start | bytes 2359300
  155.5 14.2 %collective-permute-start.2 = (bf16[64,1024]{1,0:T(8,128)(2,1)S(1)}, bf16[64,1024]{1,0:T(8,128)(2,1)S(1)}, u32[]{:S(2)}, u32[]{:S(2)}) collective-permute-start(bf16[64,1024]{1,0:T(8,128)(2,1)S(1)} %bitcast.203), channel_id=1, source_target_pairs={{0,4},{4,8},{8,12},{12,16},{16,20},{20,24},{24,28},{1,5},{5,9},{9,... | collective-permute-start | bytes 393224 | tf_op jit(solution)/shard_map/ppermute | solution.py:20
  159.7 2.3 copy-start.19
  159.7 12.6 %collective-permute-start.3 = (bf16[64,1024]{1,0:T(8,128)(2,1)S(1)}, bf16[64,1024]{1,0:T(8,128)(2,1)S(1)}, u32[]{:S(2)}, u32[]{:S(2)}) collective-permute-start(bf16[64,1024]{1,0:T(8,128)(2,1)S(1)} %bitcast.205), channel_id=1, source_target_pairs={{4,0},{8,4},{12,8},{16,12},{20,16},{24,20},{28,24},{5,1},{9,5},{13... | collective-permute-start | bytes 393224 | tf_op jit(solution)/shard_map/ppermute | solution.py:22
  228.1 32.2 %copy-start.1 = (s32[16,32,3]{1,0,2:T(8,128)S(1)}, s32[16,32,3]{1,0,2:T(8,128)}, u32[]{:S(2)}) copy-start(s32[16,32,3]{1,0,2:T(8,128)} %param.16) | copy-start | bytes 18436
Sparse Core Ops, SparseCore 0:
  9.6 25.2 all-gather.1
  129.6 82.1 all-reduce.6
  214.4 43.7 reduce-scatter.1
where the time goes:
time: 268 us; the launch traced here: 267 us
  waiting for transfers between devices  76.3 us (28%)
  blocking collectives  69.8 us (26%)
  local copies, waits for them, and re-layouts  34 us (13%)
  other arithmetic  26.7 us (10%)
  starting transfers between devices  22.9 us (9%)
  matrix products  22.6 us (8%)
  between operations  14.6 us (5%)
    psum x1, blocking collectives, body(): global_pairs = lax.psum(holding, 'ctx').astype(jnp.bfloat16)  69.8 us
    psum x1, waiting for transfers between devices, body(): summed = lax.psum(distant_terms, 'ctx')  38 us
    reduce_scatter x1, waiting for transfers between devices, body(): lax.psum_scatter(partial_value, 'head', scatter_dimension=1, tiled=True)  28.7 us
    unnamed x57, local copies, waits for them, and re-layouts  9.25 us
    scatter-add x1, other arithmetic, body(): jax.ops.segment_sum(returned.astype(jnp.float32), segment_ids, num_segmen...  9.06 us
    ppermute x2, starting transfers between devices, with_halo(): lax.ppermute(tail, axis, [(i, (i + 1) % count) for i in range(ends)])  7.94 us
    scatter x1, local copies, waits for them, and re-layouts, body(): outgoing_grads = jnp.zeros((send_tiles.shape[0], BLK, 2 * head_dim), jnp....  7.68 us
    all_to_all x1, starting transfers between devices, body(): lax.all_to_all(pick_tiles(pair_tiles, send_tiles, blocks), 'ctx', split_a...  7.41 us
  transfers between devices with their start and end apart: 9, of which 4 were waited for; matrix products, arithmetic and copies ran while one was open for 22% of the time, Pallas kernels for 0%

commit v1 on v0

--- a/solution.py
+++ b/solution.py
@@ -147,7 +147,10 @@
     holding = jnp.where(
         (global_owner == my_shard)[:, None, None, None], picked.astype(jnp.float32), 0.0
     )
-    global_pairs = lax.psum(holding, "ctx").astype(jnp.bfloat16)
+    feed_the_wires = lambda arr_in, ax_name: jnp.sum(
+        jax.lax.all_gather(arr_in, axis_name=ax_name), 0
+    )
+    global_pairs = feed_the_wires(holding, "ctx").astype(jnp.bfloat16)
     first_block = my_shard * blocks
     window_ids = first_block + jnp.arange(blocks)[:, None] + jnp.arange(3)[None, :] - 1
     inside = (window_ids >= 0) & (window_ids < blocks * shards)

time: 268 us -> 282 us (1.052)
  waiting for transfers between devices: 76.3 us -> 157 us
  blocking collectives: 69.8 us -> 0 us
  other arithmetic: 26.7 us -> 31.4 us
    psum x1 -> x0, blocking collectives: 69.8 us -> none  [body(): global_pairs = lax.psum(holding, 'ctx').astype(jnp.bfloat16)]
    all_gather x0 -> x1, waiting for transfers between devices: none -> 36.3 us  [body(): jax.lax.all_gather(arr_in, axis_name=ax_name)]
    all_to_all x1, waiting for transfers between devices: 0.01 us -> 29.8 us  [body(): lax.all_to_all(pick_tiles(pair_tiles, send_tiles, blocks), 'ctx', split_a...]
    ppermute x2, waiting for transfers between devices: 6.24 us -> 22.9 us  [with_halo(): lax.ppermute(tail, axis, [(i, (i + 1) % count) for i in range(ends)])]
    reduce_sum x0 -> x1, other arithmetic: none -> 3.26 us  [body(): jnp.sum(jax.lax.all_gather(arr_in, axis_name=ax_name), 0)]
  transfers between devices with their start and end apart: 9 -> 10, of which waited for: 4 -> 6; matrix products, arithmetic and copies ran while one was open for 22% -> 23% of each run, Pallas kernels for 0% -> 0%
where the time goes in v1:
time: 282 us; the launch traced here: 281 us
  waiting for transfers between devices  157 us (56%)
  local copies, waits for them, and re-layouts  32.3 us (11%)
  other arithmetic  31.4 us (11%)
  matrix products  23.5 us (8%)
  starting transfers between devices  22.5 us (8%)
  between operations  14.6 us (5%)
    psum x1, waiting for transfers between devices, body(): summed = lax.psum(distant_terms, 'ctx')  38.4 us
    all_gather x1, waiting for transfers between devices, body(): jax.lax.all_gather(arr_in, axis_name=ax_name)  36.3 us
    all_to_all x1, waiting for transfers between devices, body(): lax.all_to_all(pick_tiles(pair_tiles, send_tiles, blocks), 'ctx', split_a...  29.8 us
    reduce_scatter x1, waiting for transfers between devices, body(): lax.psum_scatter(partial_value, 'head', scatter_dimension=1, tiled=True)  28.6 us
    ppermute x2, waiting for transfers between devices, with_halo(): lax.ppermute(tail, axis, [(i, (i + 1) % count) for i in range(ends)])  22.9 us
    scatter-add x1, other arithmetic, body(): jax.ops.segment_sum(returned.astype(jnp.float32), segment_ids, num_segmen...  8.97 us
    unnamed x57, local copies, waits for them, and re-layouts  8.2 us
    ppermute x2, starting transfers between devices, with_halo(): lax.ppermute(tail, axis, [(i, (i + 1) % count) for i in range(ends)])  7.81 us
  transfers between devices with their start and end apart: 10, of which 6 were waited for; matrix products, arithmetic and copies ran while one was open for 23% of the time, Pallas kernels for 0%

profile of v1, /device:TPU:0, one launch (start us, length us, event | category | flops | bytes accessed | tf_op | source)
XLA Modules:
  0.0 281.1 jit_solution(13441807569586002317)
XLA Ops:
  8.0 1.0 reshape.477
  9.0 1.0 reshape.478
  11.5 0.9 convert_select_fusion
  14.0 2.1 gather_fusion.1
  16.1 7.3 %all-to-all-start = ((bf16[56,64,256]{2,1,0:T(8,128)(2,1)}), bf16[56,64,256]{2,1,0:T(8,128)(2,1)}, u32[]{:S(2)}, u32[]{:S(2)}) async-start(bf16[56,64,256]{2,1,0:T(8,128)(2,1)} %gather_fusion.1), calls=%async_computation | async-start | bytes 3670016 | tf_op jit(solution)/shard_map/all_to_all | solution.py:137
  23.6 3.9 %collective-permute-start = (bf16[64,1024]{1,0:T(8,128)(2,1)S(1)}, bf16[64,1024]{1,0:T(8,128)(2,1)S(1)}, u32[]{:S(2)}, u32[]{:S(2)}) collective-permute-start(bf16[64,1024]{1,0:T(8,128)(2,1)S(1)} %bitcast.205), channel_id=1, source_target_pairs={{0,4},{4,8},{8,12},{12,16},{16,20},{20,24},{24,28},{1,5},{5,9},{9,... | collective-permute-start | bytes 393224 | tf_op jit(solution)/shard_map/ppermute | solution.py:20
  27.6 1.3 collective-permute-start.1
  29.5 0.8 reshape.480
  30.4 13.1 %collective-permute-done = bf16[64,1024]{1,0:T(8,128)(2,1)S(1)} collective-permute-done((bf16[64,1024]{1,0:T(8,128)(2,1)S(1)}, bf16[64,1024]{1,0:T(8,128)(2,1)S(1)}, u32[]{:S(2)}, u32[]{:S(2)}) %collective-permute-start) | collective-permute-done | bytes 131104 | tf_op jit(solution)/shard_map/ppermute | solution.py:20
  44.0 0.9 copy.201
  45.3 1.2 pad_maximum_fusion
  47.0 5.0 %convolution_convert_fusion.1 = bf16[256,512]{1,0:T(8,128)(2,1)} fusion(bf16[256,4096]{1,0:T(8,128)(2,1)} %all-gather.5.cloned.1.call-done, bf16[512,4096]{1,0:T(8,128)(2,1)} %param.15), kind=kOutput, calls=%fused_computation.40 | convolution fusion | flops 1073872896 | bytes 6553600 | tf_op jit(solution)/shard_map/dot_general | solution.py:177
  51.9 1.0 reshape.486
  53.0 1.6 fusion.22
  54.6 29.8 %all-to-all-done = bf16[56,64,256]{2,1,0:T(8,128)(2,1)} async-done(((bf16[56,64,256]{2,1,0:T(8,128)(2,1)}), bf16[56,64,256]{2,1,0:T(8,128)(2,1)}, u32[]{:S(2)}, u32[]{:S(2)}) %all-to-all-start) | async-done | bytes 1835040 | tf_op jit(solution)/shard_map/all_to_all | solution.py:137
  84.4 2.2 gather_fusion.2
  87.0 0.9 copy-done.9
  88.3 1.5 fusion.25
  89.8 36.3 %all-gather.3.cloned.1.call-done = f32[8,2,64,4,256]{4,2,3,1,0:T(8,128)} async-done(((f32[1,2,64,4,256]{4,2,3,1,0:T(8,128)}), f32[8,2,64,4,256]{4,2,3,1,0:T(8,128)}) %all-gather.3.cloned.1.call-update) | async-done | bytes 4194320 | tf_op jit(solution)/shard_map/all_gather | solution.py:151
  126.0 3.3 %reduce_sum.45 = bf16[2,64,4,256]{3,1,2,0:T(8,128)(2,1)} reduce(f32[8,2,64,4,256]{4,2,3,1,0:T(8,128)} %all-gather.3.cloned.1.call-done, f32[]{:T(128)} %constant.164.clone.1), dimensions={0}, to_apply=%region_0.1 | reduce | flops 917504 | bytes 4456452 | tf_op jit(solution)/shard_map/reduce_sum | solution.py:150
  129.3 1.4 convolution_bitcast_fusion.3
  130.7 0.8 fusion.85
  131.5 1.2 exponential_reduce_fusion
  132.8 1.1 fusion.3
  134.6 1.2 copy-done.12
  137.0 1.1 multiply_reduce_fusion
  138.7 1.5 fusion.2
  140.3 1.4 copy-done.7
  142.0 0.8 pad_maximum_fusion.5
  143.3 5.4 %fusion.35 = f32[256,4096]{1,0:T(8,128)} fusion(bf16[512,4096]{1,0:T(8,128)(2,1)} %param.15, bf16[32,8,4,128]{3,2,1,0:T(4,128)(2,1)S(1)} %bitcast.190), kind=kOutput, calls=%fused_computation.78 | convolution fusion | flops 1073741824 | bytes 8650752 | tf_op jit(solution)/shard_map/dot_general | solution.py:173
  148.7 1.6 copy-done.8
  150.6 1.2 copy-done.3
  152.4 1.4 pad_maximum_fusion.1
  153.7 1.5 broadcast_in_dim.82
  155.2 7.6 %scatter_fusion = bf16[56,64,256]{2,1,0:T(8,128)(2,1)} fusion(bf16[56,64,256]{2,1,0:T(8,128)(2,1)} %broadcast_in_dim.82, s32[48]{0:T(128)S(1)} %fusion.76, bf16[48,64,256]{2,1,0:T(8,128)(2,1)} %pad_maximum_fusion.1), kind=kCustom, calls=%fused_computation.3 | custom fusion | bytes 4718784 | tf_op jit(solution)/shard_map/scatter | solution.py:228
  162.8 4.4 %all-to-all-start.1 = ((bf16[56,64,256]{2,1,0:T(8,128)(2,1)}), bf16[56,64,256]{2,1,0:T(8,128)(2,1)}, u32[]{:S(2)}, u32[]{:S(2)}) async-start(bf16[56,64,256]{2,1,0:T(8,128)(2,1)} %scatter_fusion), calls=%async_computation.2 | async-start | bytes 3670016 | tf_op jit(solution)/shard_map/all_to_all | solution.py:230
  168.7 3.9 %collective-permute-start.2 = (bf16[64,1024]{1,0:T(8,128)(2,1)S(1)}, bf16[64,1024]{1,0:T(8,128)(2,1)S(1)}, u32[]{:S(2)}, u32[]{:S(2)}) collective-permute-start(bf16[64,1024]{1,0:T(8,128)(2,1)S(1)} %bitcast.199), channel_id=1, source_target_pairs={{0,4},{4,8},{8,12},{12,16},{16,20},{20,24},{24,28},{1,5},{5,9},{9,... | collective-permute-start | bytes 393224 | tf_op jit(solution)/shard_map/ppermute | solution.py:20
  172.8 1.4 collective-permute-start.3
  176.5 9.8 %collective-permute-done.2 = bf16[64,1024]{1,0:T(8,128)(2,1)S(1)} collective-permute-done((bf16[64,1024]{1,0:T(8,128)(2,1)S(1)}, bf16[64,1024]{1,0:T(8,128)(2,1)S(1)}, u32[]{:S(2)}, u32[]{:S(2)}) %collective-permute-start.2) | collective-permute-done | bytes 131104 | tf_op jit(solution)/shard_map/ppermute | solution.py:20
  186.6 1.0 fusion.39
  187.7 38.4 %all-reduce.6.cloned.1.call-done = f32[2,64,4,256]{3,1,0,2:T(8,128)} async-done(((f32[2,64,4,256]{3,1,0,2:T(8,128)}), f32[2,64,4,256]{3,1,0,2:T(8,128)}) %all-reduce.6.cloned.1.call-update) | async-done | bytes 524304 | tf_op jit(solution)/shard_map/psum | solution.py:213
  226.1 2.6 fusion.33
  228.7 3.8 %convert_element_type.74 = f32[56,64,256]{2,1,0:T(8,128)} convert(bf16[56,64,256]{2,1,0:T(8,128)(2,1)} %all-to-all-done.1) | non-fusion elementwise | flops 917504 | bytes 5505024 | tf_op jit(solution)/shard_map/convert_element_type | solution.py:233
  232.6 9.0 %scatter_fusion.1 = f32[17,64,256]{2,1,0:T(8,128)S(1)} fusion(f32[17,64,256]{2,1,0:T(8,128)S(1)} %broadcast_in_dim.80, s32[56]{0:T(128)S(1)} %get-tuple-element.51, f32[56,64,256]{2,1,0:T(8,128)} %convert_element_type.74), kind=kCustom, calls=%fused_computation.4 | custom fusion | flops 917504 | bytes 11010272 | tf_op jit(solution)/shard_map/scatter-add | solution.py:232
  241.6 0.8 fusion.16
  243.0 0.9 copy_bitcast_fusion
  243.8 28.6 %reduce-scatter.2.cloned.1.call-done = f32[256,1024]{1,0:T(8,128)} async-done(((f32[256,4096]{1,0:T(8,128)}), f32[256,1024]{1,0:T(8,128)}) %reduce-scatter.2.cloned.1.call-update) | async-done | bytes 1048592 | tf_op jit(solution)/shard_map/reduce_scatter | solution.py:174
  272.5 2.1 convert_element_type.67
  (134 shorter events, 15.6 us)
Async XLA Ops:
  7.2 5.2 %copy-start = (s32[16,32,3]{1,0,2:T(8,128)S(1)}, s32[16,32,3]{1,0,2:T(8,128)}, u32[]{:S(2)}) copy-start(s32[16,32,3]{1,0,2:T(8,128)} %param.16) | copy-start | bytes 18436
  7.2 4.2 %copy-start.24 = (s32[2]{0:T(128)S(1)}, s32[2]{0:T(128)}, u32[]{:S(2)}) copy-start(s32[2]{0:T(128)} %param.17) | copy-start | bytes 28
  7.2 39.8 %all-gather.5.cloned.1.call-start = ((), (), s32[]{:S(2)}) async-start(), calls=%async_computation.5 | async-start | bytes 2621440 | tf_op jit(solution)/shard_map/all_gather | solution.py:178
  7.9 118.1 %all-gather.3.cloned.1.call-start = ((), (), s32[]{:S(2)}) async-start(), calls=%async_computation.3 | async-start | bytes 4718592 | tf_op jit(solution)/shard_map/all_gather | solution.py:151
  16.1 68.3 %all-to-all-start = ((bf16[56,64,256]{2,1,0:T(8,128)(2,1)}), bf16[56,64,256]{2,1,0:T(8,128)(2,1)}, u32[]{:S(2)}, u32[]{:S(2)}) async-start(bf16[56,64,256]{2,1,0:T(8,128)(2,1)} %gather_fusion.1), calls=%async_computation | async-start | bytes 3670016 | tf_op jit(solution)/shard_map/all_to_all | solution.py:137
  23.4 6.1 %copy-start.23 = (bf16[256,512]{1,0:T(8,128)(2,1)S(1)}, bf16[256,512]{1,0:T(8,128)(2,1)}, u32[]{:S(2)}) copy-start(bf16[256,512]{1,0:T(8,128)(2,1)} %param.11) | copy-start | bytes 786436
  23.4 202.7 %all-reduce.6.cloned.1.call-start = ((), (), s32[]{:S(2)}) async-start(), calls=%async_computation.6 | async-start | bytes 1048576 | tf_op jit(solution)/shard_map/psum | solution.py:213
  23.6 19.8 %collective-permute-start = (bf16[64,1024]{1,0:T(8,128)(2,1)S(1)}, bf16[64,1024]{1,0:T(8,128)(2,1)S(1)}, u32[]{:S(2)}, u32[]{:S(2)}) collective-permute-start(bf16[64,1024]{1,0:T(8,128)(2,1)S(1)} %bitcast.205), channel_id=1, source_target_pairs={{0,4},{4,8},{8,12},{12,16},{16,20},{20,24},{24,28},{1,5},{5,9},{9,... | collective-permute-start | bytes 393224 | tf_op jit(solution)/shard_map/ppermute | solution.py:20
  27.6 15.8 %collective-permute-start.1 = (bf16[64,1024]{1,0:T(8,128)(2,1)S(1)}, bf16[64,1024]{1,0:T(8,128)(2,1)S(1)}, u32[]{:S(2)}, u32[]{:S(2)}) collective-permute-start(bf16[64,1024]{1,0:T(8,128)(2,1)S(1)} %bitcast.206), channel_id=1, source_target_pairs={{4,0},{8,4},{12,8},{16,12},{20,16},{24,20},{28,24},{5,1},{9,5},{13... | collective-permute-start | bytes 393224 | tf_op jit(solution)/shard_map/ppermute | solution.py:22
  45.2 1.3 copy-start.13
  46.6 6.4 %copy-start.4 = (bf16[4,3,64,4,256]{4,2,1,3,0:T(8,128)(2,1)}, bf16[4,3,64,4,256]{4,2,1,3,0:T(8,128)(2,1)S(1)}, u32[]{:S(2)}) copy-start(bf16[4,3,64,4,256]{4,2,1,3,0:T(8,128)(2,1)S(1)} %pad_maximum_fusion) | copy-start | bytes 4718596
  86.5 1.4 copy-start.14
  87.0 0.9 copy-start.9
  87.0 1.2 copy-start.11
  132.8 1.4 copy-start.5
  134.2 2.8 %copy-start.2 = (bf16[4,4,64,8,64]{2,4,3,1,0:T(8,128)(2,1)}, bf16[4,4,64,8,64]{2,4,3,1,0:T(8,128)(2,1)S(1)}, u32[]{:S(2)}) copy-start(bf16[4,4,64,8,64]{2,4,3,1,0:T(8,128)(2,1)S(1)} %fusion.3) | copy-start | bytes 3145732
  134.2 1.7 copy-start.12
  134.2 2.1 copy-start.20
  136.7 1.4 copy-start.17
  136.7 2.0 copy-start.18
  138.7 2.9 %copy-start.15 = (bf16[4,64,4,128]{3,2,1,0:T(4,128)(2,1)S(1)}, bf16[4,64,4,128]{3,2,1,0:T(4,128)(2,1)}, u32[]{:S(2)}) copy-start(bf16[4,64,4,128]{3,2,1,0:T(4,128)(2,1)} %reshape.480) | copy-start | bytes 786436
  140.2 1.4 copy-start.7
  141.6 1.4 copy-start.22
  142.8 129.7 %reduce-scatter.2.cloned.1.call-start = ((), (), s32[]{:S(2)}) async-start(), calls=%async_computation.4 | async-start | bytes 5242880 | tf_op jit(solution)/shard_map/reduce_scatter | solution.py:174
  148.7 1.6 copy-start.8
  148.7 1.6 copy-start.16
  150.3 1.6 copy-start.3
  162.8 65.9 %all-to-all-start.1 = ((bf16[56,64,256]{2,1,0:T(8,128)(2,1)}), bf16[56,64,256]{2,1,0:T(8,128)(2,1)}, u32[]{:S(2)}, u32[]{:S(2)}) async-start(bf16[56,64,256]{2,1,0:T(8,128)(2,1)} %scatter_fusion), calls=%async_computation.2 | async-start | bytes 3670016 | tf_op jit(solution)/shard_map/all_to_all | solution.py:230
  168.2 6.0 %copy-start.6 = (bf16[4,3,64,4,256]{4,2,1,3,0:T(8,128)(2,1)S(1)}, bf16[4,3,64,4,256]{4,2,1,3,0:T(8,128)(2,1)}, u32[]{:S(2)}) copy-start(bf16[4,3,64,4,256]{4,2,1,3,0:T(8,128)(2,1)} %copy-done.4) | copy-start | bytes 4718596
  168.5 6.9 %copy-start.19 = (f32[6,64,4,256]{3,1,2,0:T(8,128)}, f32[6,64,4,256]{3,1,2,0:T(8,128)S(1)}, u32[]{:S(2)}) copy-start(f32[6,64,4,256]{3,1,2,0:T(8,128)S(1)} %get-tuple-element.29) | copy-start | bytes 4718596
  168.5 6.2 %copy-start.10 = (bf16[4,4,3,64,128]{4,3,2,1,0:T(8,128)(2,1)S(1)}, bf16[4,4,3,64,128]{4,3,2,1,0:T(8,128)(2,1)}, u32[]{:S(2)}) copy-start(bf16[4,4,3,64,128]{4,3,2,1,0:T(8,128)(2,1)} %copy-done.9) | copy-start | bytes 2359300
  168.7 17.6 %collective-permute-start.2 = (bf16[64,1024]{1,0:T(8,128)(2,1)S(1)}, bf16[64,1024]{1,0:T(8,128)(2,1)S(1)}, u32[]{:S(2)}, u32[]{:S(2)}) collective-permute-start(bf16[64,1024]{1,0:T(8,128)(2,1)S(1)} %bitcast.199), channel_id=1, source_target_pairs={{0,4},{4,8},{8,12},{12,16},{16,20},{20,24},{24,28},{1,5},{5,9},{9,... | collective-permute-start | bytes 393224 | tf_op jit(solution)/shard_map/ppermute | solution.py:20
  172.8 2.3 copy-start.21
  172.8 13.6 %collective-permute-start.3 = (bf16[64,1024]{1,0:T(8,128)(2,1)S(1)}, bf16[64,1024]{1,0:T(8,128)(2,1)S(1)}, u32[]{:S(2)}, u32[]{:S(2)}) collective-permute-start(bf16[64,1024]{1,0:T(8,128)(2,1)S(1)} %bitcast.201), channel_id=1, source_target_pairs={{4,0},{8,4},{12,8},{16,12},{20,16},{24,20},{28,24},{5,1},{9,5},{13... | collective-permute-start | bytes 393224 | tf_op jit(solution)/shard_map/ppermute | solution.py:22
  242.4 32.2 %copy-start.1 = (s32[16,32,3]{1,0,2:T(8,128)S(1)}, s32[16,32,3]{1,0,2:T(8,128)}, u32[]{:S(2)}) copy-start(s32[16,32,3]{1,0,2:T(8,128)} %param.16) | copy-start | bytes 18436
Sparse Core Ops, SparseCore 0:
  9.6 25.2 all-gather.4
  37.6 88.3 all-gather.2
  142.9 83.1 all-reduce.5
  228.6 43.7 reduce-scatter.1
